TPU v7x, 256 devices: a whole 4x4x8 slice. The times are simulated.
256 devices in a mesh: date: 64 (over x, z_lo, y), strip: 4 (over z_hi, core).
Axes of the slice: x: 4, y: 4, z: 8 (z_hi: 2, z_lo: 4; z = z_hi * 4 + z_lo), core: 2. Of those that a mesh axis runs over, the one named last changes fastest.
Arguments:
- slc: bfloat16 [2, 256, 512, 2048], P(None, 'date', 'strip'), may hold values from -40 to 40, as said below
- partner_offset: int32 [256, 4], P('date'), may hold values from -4 to 4, as said below
Outputs:
- interferogram: float32 [256, 4, 2, 128, 128], P('date', None, None, 'strip')
- coherence: float32 [256, 4, 128, 128], P('date', None, 'strip')
Inputs may be any that keep to these rules, and one draw needn't show every extreme that they name: `slc`: complex samples as real and imaginary parts. `partner_offset`: each date's 4 offsets are nonzero and of distinct magnitudes, and date + offset lies in 0 to 255.
All inputs are finite; a program needn't handle non-finite values.
Results may differ from a plain program's by a relative error of at most 0.0003.
Values may be sent and summed in bfloat16 or wider, within the bound.
A program may use at most 128 MiB of HBM per device.

v0:
```python
import jax
import jax.numpy as jnp
from jax import lax
from jax.sharding import PartitionSpec as P

DATE_DEV = 4
PARTNERS = 4
MAXOFF = 4
LOOK_AZ = 4
LOOK_RG = 16


EPS = 1e-06


def extended_2(block, sides, width):
    for axis, dim in sides:
        count = lax.axis_size(axis)
        forward = [(i, i + 1) for i in range(count - 1)]
        backward = [(target, source) for source, target in forward]
        low = lax.ppermute(
            lax.slice_in_dim(block, block.shape[dim] - width, None, axis=dim), axis, forward
        )
        high = lax.ppermute(lax.slice_in_dim(block, 0, width, axis=dim), axis, backward)
        block = jnp.concatenate([low, block, high], axis=dim)
    return block


def passed_along(block, axis, distance):
    devices = range(lax.axis_size(axis))
    route = [(i - distance, i) for i in devices if i - distance in devices]
    return lax.ppermute(block, axis, route)


def range_sum(values):
    cells = values.shape[-1]
    cell_group = jnp.arange(cells, dtype=jnp.int32)[:, None] // LOOK_RG
    look_index = jnp.arange(cells // LOOK_RG, dtype=jnp.int32)[None, :]
    selector = (cell_group == look_index).astype(jnp.float32)
    return jnp.dot(
        values, selector, precision=lax.Precision.HIGHEST, preferred_element_type=jnp.float32
    )


def look_sums(own_tile, partner_tile):
    own_real = own_tile[0].astype(jnp.float32)[..., None, :, :]
    own_imag = own_tile[1].astype(jnp.float32)[..., None, :, :]
    far_real = partner_tile[0].astype(jnp.float32)
    far_imag = partner_tile[1].astype(jnp.float32)
    prod_real = range_sum(own_real * far_real + own_imag * far_imag)
    prod_imag = range_sum(own_imag * far_real - own_real * far_imag)
    own_power = jnp.broadcast_to(
        range_sum(own_real * own_real + own_imag * own_imag), prod_real.shape
    )
    far_power = range_sum(far_real * far_real + far_imag * far_imag)
    return jnp.stack([prod_real, prod_imag, own_power, far_power], axis=-3)


def finish(extended):
    margin = LOOK_AZ // 2
    total_rows = extended.shape[-2]
    columns = extended.shape[-1]
    inner_rows = extended[..., margin : total_rows - margin, :]
    leading = inner_rows.shape[:-2]
    looks = inner_rows.reshape(leading + (inner_rows.shape[-2] // LOOK_AZ, LOOK_AZ, columns)).sum(
        -2
    )
    interferogram = looks[..., 0:2, :, :] / float(LOOK_AZ * LOOK_RG)
    blocks = extended.reshape(leading + (total_rows // LOOK_AZ, LOOK_AZ, columns)).sum(-2)
    windows = blocks[..., :-1, :] + blocks[..., 1:, :]
    magnitude = jnp.sqrt(
        windows[..., 0, :, :] * windows[..., 0, :, :]
        + windows[..., 1, :, :] * windows[..., 1, :, :]
    )
    coherence = magnitude / jnp.sqrt(windows[..., 2, :, :] * windows[..., 3, :, :] + EPS)
    return (interferogram, coherence)


def per_device(slc, partner_offset):
    reach = (MAXOFF + DATE_DEV - 1) // DATE_DEV
    margin = LOOK_AZ // 2
    own_tile = extended_2(slc, (("strip", 2),), margin)
    fetched = {}
    for heading in (1, -1):
        fetched[heading] = passed_along(own_tile, "date", -heading * 1)
    ordered = [fetched[-1]] + [own_tile] + [fetched[1]]
    window = jnp.concatenate(ordered, axis=1)
    local_index = jnp.arange(DATE_DEV, dtype=jnp.int32)[:, None] + partner_offset + reach * DATE_DEV
    partner_tile = jnp.take(window, local_index.reshape(-1), axis=1)
    partner_tile = partner_tile.reshape((2, DATE_DEV, PARTNERS) + partner_tile.shape[2:])
    sums = look_sums(own_tile, partner_tile)
    return finish(sums)


def solution(mesh):
    return jax.shard_map(
        per_device,
        mesh=mesh,
        in_specs=(P(None, "date", "strip", None), P("date", None)),
        out_specs=(P("date", None, None, "strip", None), P("date", None, "strip", None)),
        check_vma=False,
    )
```

profile of v0, /device:TPU:5, one launch (start us, length us, event | category | flops | bytes accessed | tf_op | source)
XLA Modules:
  0.0 218.7 jit_solution(10811786673708685131)
XLA Ops:
  0.6 1.1 fusion.42
  1.8 0.0 copy-start.1
  1.8 9.4 %collective-permute-start = (bf16[2,4,2,2048]{3,2,1,0:T(2,128)(2,1)S(1)}, bf16[2,4,2,2048]{3,2,1,0:T(2,128)(2,1)S(1)}, u32[]{:S(2)}, u32[]{:S(2)}) collective-permute-start(bf16[2,4,2,2048]{3,2,1,0:T(2,128)(2,1)S(1)} %get-tuple-element.8), channel_id=1, source_target_pairs={{0,1},{1,2},{2,3},{4,5},{5,6},{6,7},{8,9},{9,10},{10,11},{12,13},{... | collective-permute-start | bytes 196616 | tf_op jit(solution)/shard_map/ppermute | solution.py:21
  11.2 1.9 collective-permute-start.1
  13.1 0.0 collective-permute-done
  13.1 7.6 %collective-permute-done.1 = bf16[2,4,2,2048]{3,2,1,0:T(2,128)(2,1)S(1)} collective-permute-done((bf16[2,4,2,2048]{3,2,1,0:T(2,128)(2,1)S(1)}, bf16[2,4,2,2048]{3,2,1,0:T(2,128)(2,1)S(1)}, u32[]{:S(2)}, u32[]{:S(2)}) %collective-permute-start.1) | collective-permute-done | bytes 65568 | tf_op jit(solution)/shard_map/ppermute | solution.py:24
  20.7 4.7 %pad_maximum_fusion.1 = bf16[2,4,132,2048]{3,2,1,0:T(8,128)(2,1)} fusion(bf16[2,4,2,2048]{3,2,1,0:T(2,128)(2,1)S(1)} %collective-permute-done.1, bf16[2,4,128,2048]{3,2,1,0:T(8,128)(2,1)} %param.2, bf16[2,4,2,2048]{3,2,1,0:T(2,128)(2,1)S(1)} %collective-permute-done), kind=kLoop, calls=%fused_computation.19 | loop fusion | flops 12976128 | bytes 8650752 | tf_op jit(solution)/shard_map/concatenate | solution.py:25
  25.4 3.2 %collective-permute-start.2 = (bf16[2,4,132,2048]{3,2,1,0:T(8,128)(2,1)}, bf16[2,4,132,2048]{3,2,1,0:T(8,128)(2,1)}, u32[]{:S(2)}, u32[]{:S(2)}) collective-permute-start(bf16[2,4,132,2048]{3,2,1,0:T(8,128)(2,1)} %pad_maximum_fusion.1), channel_id=1, source_target_pairs={{0,4},{4,8},{8,12},{12,16},{16,20},{20,24},{24,28},{28,32},{32,36}... | collective-permute-start | bytes 12976136 | tf_op jit(solution)/shard_map/ppermute | solution.py:32
  28.6 6.9 %collective-permute-start.3 = (bf16[2,4,132,2048]{3,2,1,0:T(8,128)(2,1)}, bf16[2,4,132,2048]{3,2,1,0:T(8,128)(2,1)}, u32[]{:S(2)}, u32[]{:S(2)}) collective-permute-start(bf16[2,4,132,2048]{3,2,1,0:T(8,128)(2,1)} %pad_maximum_fusion.1), channel_id=1, source_target_pairs={{4,0},{8,4},{12,8},{16,12},{20,16},{24,20},{28,24},{32,28},{36,32}... | collective-permute-start | bytes 12976136 | tf_op jit(solution)/shard_map/ppermute | solution.py:32
  35.5 0.0 copy-done.1
  35.5 0.1 reshape.134
  35.6 0.1 reshape.133
  35.7 5.2 %fusion.13 = f32[4,132,128]{2,1,0:T(8,128)S(1)} fusion(bf16[2,4,132,2048]{3,2,1,0:T(8,128)(2,1)} %pad_maximum_fusion.1, s32[2048]{0:T(1024)S(1)} %add_select_fusion), kind=kOutput, calls=%fused_computation.20 | convolution fusion | flops 1666613248 | bytes 4603904 | tf_op jit(solution)/shard_map/dot_general | solution.py:40
  40.9 0.1 copy.11
  41.0 0.1 copy.12
  41.1 0.0 copy-start
  41.1 7.0 %fusion.18 = (f32[4,132,2048]{2,1,0:T(8,128)}, f32[4,132,2048]{2,1,0:T(8,128)}) fusion(bf16[2,4,132,2048]{3,2,1,0:T(8,128)(2,1)} %pad_maximum_fusion.1), kind=kLoop, calls=%fused_computation.31 | loop fusion | flops 2162688 | bytes 12976128 | tf_op jit(solution)/shard_map/convert_element_type | solution.py:46
  48.1 76.3 %collective-permute-done.2 = bf16[2,4,132,2048]{3,2,1,0:T(8,128)(2,1)} collective-permute-done((bf16[2,4,132,2048]{3,2,1,0:T(8,128)(2,1)}, bf16[2,4,132,2048]{3,2,1,0:T(8,128)(2,1)}, u32[]{:S(2)}, u32[]{:S(2)}) %collective-permute-start.2) | collective-permute-done | bytes 4325408 | tf_op jit(solution)/shard_map/ppermute | solution.py:32
  124.4 1.8 collective-permute-done.3
  126.2 0.0 copy-done
  126.2 10.8 %pad_maximum_fusion = bf16[2,12,132,2048]{3,2,1,0:T(8,128)(2,1)} fusion(bf16[2,4,132,2048]{3,2,1,0:T(8,128)(2,1)} %collective-permute-done.3, bf16[2,4,2,2048]{3,2,1,0:T(2,128)(2,1)S(1)} %collective-permute-done.1, bf16[2,4,128,2048]{3,2,1,0:T(8,128)(2,1)S(1)} %copy-done, bf16[2,4,2,2048]{3,2,1,0:T(2,128)(2,1)S(1)} %collective-permute-done, ...), kind=kLoop, calls=%fused_computation.14 | loop fusion | flops 64880640 | bytes 25952256 | tf_op jit(solution)/shard_map/concatenate | solution.py:87
  137.0 12.4 %gather_fusion = bf16[16,2,132,2048]{3,2,1,0:T(8,128)(2,1)} fusion(bf16[2,12,132,2048]{3,2,1,0:T(8,128)(2,1)} %pad_maximum_fusion, s32[1024]{0:T(1024)S(1)} %pad_clamp_fusion), kind=kCustom, calls=%fused_computation | custom fusion | bytes 34603072 | tf_op jit(solution)/shard_map/jit(_take)/gather | solution.py:89
  149.4 8.8 %select_bitcast_fusion = bf16[2,16,132,2048]{3,2,0,1:T(8,128)(2,1)S(1)} fusion(bf16[16,2,132,2048]{3,2,1,0:T(8,128)(2,1)} %gather_fusion, pred[16]{0:T(512)(128)(4,1)S(1)} %compare_and_fusion), kind=kLoop, calls=%fused_computation.13 | loop fusion | flops 8650752 | bytes 34603024 | tf_op jit(solution)/shard_map/jit(_take)/select_n | solution.py:89
  158.2 4.2 %fusion.41 = (bf16[1,16,132,2048]{3,2,0,1:T(8,128)(2,1)S(1)}, bf16[1,16,132,2048]{3,2,0,1:T(8,128)(2,1)}) fusion(bf16[2,16,132,2048]{3,2,0,1:T(8,128)(2,1)S(1)} %select_bitcast_fusion), kind=kLoop, calls=%fused_computation.63 | loop fusion | bytes 34603008 | tf_op jit(solution)/shard_map/slice | solution.py:49
  162.4 14.7 %fusion.1 = f32[4,4,132,128]{3,2,1,0:T(8,128)S(1)} fusion(bf16[4,4,132,2048]{3,2,1,0:T(8,128)(2,1)} %bitcast.47, bf16[4,4,132,2048]{3,2,1,0:T(8,128)(2,1)S(1)} %bitcast.44, f32[4,132,2048]{2,1,0:T(8,128)} %get-tuple-element.7, f32[4,132,2048]{2,1,0:T(8,128)} %get-tuple-element.6, s32[2048]{0:T(1024)S(1)} %add_select_fusion), kind=kOutput, calls=%fused_computation.8 | convolution fusion | flops 6665666560 | bytes 27041792 | tf_op jit(solution)/shard_map/dot_general | solution.py:40
  177.1 14.9 %fusion.4 = f32[4,4,132,128]{3,2,1,0:T(8,128)S(1)} fusion(bf16[4,4,132,2048]{3,2,1,0:T(8,128)(2,1)} %bitcast.48, bf16[4,4,132,2048]{3,2,1,0:T(8,128)(2,1)S(1)} %bitcast.45, f32[4,132,2048]{2,1,0:T(8,128)} %get-tuple-element.7, f32[4,132,2048]{2,1,0:T(8,128)} %get-tuple-element.6, s32[2048]{0:T(1024)S(1)} %add_select_fusion), kind=kOutput, calls=%fused_computation.10 | convolution fusion | flops 6665666560 | bytes 27041792 | tf_op jit(solution)/shard_map/dot_general | solution.py:40
  192.1 13.6 %fusion.7 = f32[4,4,132,128]{3,2,1,0:T(8,128)S(1)} fusion(bf16[4,4,132,2048]{3,2,1,0:T(8,128)(2,1)} %bitcast.49, bf16[4,4,132,2048]{3,2,1,0:T(8,128)(2,1)S(1)} %bitcast.46, s32[2048]{0:T(1024)S(1)} %add_select_fusion), kind=kOutput, calls=%fused_computation.12 | convolution fusion | flops 6665666560 | bytes 18391040 | tf_op jit(solution)/shard_map/dot_general | solution.py:40
  205.6 0.3 copy.9
  205.9 0.3 copy.10
  206.2 0.3 copy.13
  206.5 0.2 stack_broadcast_in_dim.11
  206.7 2.3 %maximum_reduce_fusion = f32[4,4,4,33,128]{4,1,3,0,2:T(4,128)S(1)} fusion(f32[4,4,1,33,4,128]{5,1,4,3,0,2:T(4,128)S(1)} %bitcast.56, f32[4,4,1,33,4,128]{5,1,4,3,0,2:T(4,128)S(1)} %stack_broadcast_in_dim.11, f32[4,4,1,33,4,128]{5,1,4,3,0,2:T(4,128)S(1)} %bitcast.55, f32[4,4,1,33,4,128]{5,1,4,3,0,2:T(4,128)S(1)} %bitcast.54), kind=kLoop, calls=%fused_computation.24 | loop fusion | flops 4055040 | bytes 5406720 | tf_op jit(solution)/shard_map/reduce_sum | solution.py:69
  209.0 0.3 slice_add_fusion
  209.3 0.2 fusion.34
  209.5 0.7 copy.15
  210.3 0.1 stack_broadcast_in_dim.9
  210.3 2.6 %pad_maximum_fusion.2 = f32[4,4,4,128,128]{4,3,1,0,2:T(8,128)} fusion(f32[4,4,1,132,128]{4,3,1,0,2:T(8,128)S(1)} %bitcast.53, f32[4,4,1,132,128]{4,3,1,0,2:T(8,128)S(1)} %stack_broadcast_in_dim.9, f32[4,4,1,132,128]{4,3,1,0,2:T(8,128)S(1)} %bitcast.52, f32[4,4,1,132,128]{4,3,1,0,2:T(8,128)S(1)} %bitcast.51), kind=kLoop, calls=%fused_computation.25 | loop fusion | flops 3145728 | bytes 8519680 | tf_op jit(solution)/shard_map/stack | solution.py:56
  212.9 4.8 %reduce_sum.18 = f32[4,4,4,32,128]{4,3,1,0,2:T(8,128)S(1)} reduce(f32[4,4,4,32,4,128]{5,4,3,1,0,2:T(4,128)} %bitcast.50, f32[]{:T(128)} %constant.44.clone.1), dimensions={4}, to_apply=%region_0.1 | reduce | flops 786432 | bytes 5242884 | tf_op jit(solution)/shard_map/reduce_sum | solution.py:65
  217.8 0.8 copy.14
  (6 shorter events, 0.1 us)
Async XLA Ops:
  1.8 33.7 %copy-start.1 = (s32[4,4]{1,0:T(4,128)S(1)}, s32[4,4]{1,0:T(4,128)}, u32[]{:S(2)}) copy-start(s32[4,4]{1,0:T(4,128)} %param.3) | copy-start | bytes 196
  1.8 11.3 %collective-permute-start = (bf16[2,4,2,2048]{3,2,1,0:T(2,128)(2,1)S(1)}, bf16[2,4,2,2048]{3,2,1,0:T(2,128)(2,1)S(1)}, u32[]{:S(2)}, u32[]{:S(2)}) collective-permute-start(bf16[2,4,2,2048]{3,2,1,0:T(2,128)(2,1)S(1)} %get-tuple-element.8), channel_id=1, source_target_pairs={{0,1},{1,2},{2,3},{4,5},{5,6},{6,7},{8,9},{9,10},{10,11},{12,13},{... | collective-permute-start | bytes 196616 | tf_op jit(solution)/shard_map/ppermute | solution.py:21
  11.2 9.5 %collective-permute-start.1 = (bf16[2,4,2,2048]{3,2,1,0:T(2,128)(2,1)S(1)}, bf16[2,4,2,2048]{3,2,1,0:T(2,128)(2,1)S(1)}, u32[]{:S(2)}, u32[]{:S(2)}) collective-permute-start(bf16[2,4,2,2048]{3,2,1,0:T(2,128)(2,1)S(1)} %get-tuple-element.9), channel_id=1, source_target_pairs={{1,0},{2,1},{3,2},{5,4},{6,5},{7,6},{9,8},{10,9},{11,10},{13,12},{... | collective-permute-start | bytes 196616 | tf_op jit(solution)/shard_map/ppermute | solution.py:24
  25.4 99.0 %collective-permute-start.2 = (bf16[2,4,132,2048]{3,2,1,0:T(8,128)(2,1)}, bf16[2,4,132,2048]{3,2,1,0:T(8,128)(2,1)}, u32[]{:S(2)}, u32[]{:S(2)}) collective-permute-start(bf16[2,4,132,2048]{3,2,1,0:T(8,128)(2,1)} %pad_maximum_fusion.1), channel_id=1, source_target_pairs={{0,4},{4,8},{8,12},{12,16},{16,20},{20,24},{24,28},{28,32},{32,36}... | collective-permute-start | bytes 12976136 | tf_op jit(solution)/shard_map/ppermute | solution.py:32
  28.6 97.6 %collective-permute-start.3 = (bf16[2,4,132,2048]{3,2,1,0:T(8,128)(2,1)}, bf16[2,4,132,2048]{3,2,1,0:T(8,128)(2,1)}, u32[]{:S(2)}, u32[]{:S(2)}) collective-permute-start(bf16[2,4,132,2048]{3,2,1,0:T(8,128)(2,1)} %pad_maximum_fusion.1), channel_id=1, source_target_pairs={{4,0},{8,4},{12,8},{16,12},{20,16},{24,20},{28,24},{32,28},{36,32}... | collective-permute-start | bytes 12976136 | tf_op jit(solution)/shard_map/ppermute | solution.py:32
  41.1 85.1 %copy-start = (bf16[2,4,128,2048]{3,2,1,0:T(8,128)(2,1)S(1)}, bf16[2,4,128,2048]{3,2,1,0:T(8,128)(2,1)}, u32[]{:S(2)}) copy-start(bf16[2,4,128,2048]{3,2,1,0:T(8,128)(2,1)} %param.2) | copy-start | bytes 12582916
where the time goes:
time: 219 us
  waiting for transfers between devices  85.6 us (39%)
  matrix products  48.4 us (22%)
  other arithmetic  41.6 us (19%)
  starting transfers between devices  21.4 us (10%)
  local copies, waits for them, and re-layouts  20.7 us (9%)
    ppermute x2, waiting for transfers between devices, passed_along(): return lax.ppermute(block, axis, route)  78.1 us
    dot_general x4, matrix products, range_sum(): jnp.dot(values, selector, precision=lax.Precision.HIGHEST, preferred_elem...  48.4 us
    gather x1, local copies, waits for them, and re-layouts, per_device(): partner_tile = jnp.take(window, local_index.reshape(-1), axis=1)  12.4 us
    concatenate x1, other arithmetic, per_device(): window = jnp.concatenate(ordered, axis=1)  10.8 us
    ppermute x2, starting transfers between devices, passed_along(): return lax.ppermute(block, axis, route)  10.1 us
    ppermute x1, starting transfers between devices, extended_2(): lax.ppermute(lax.slice_in_dim(block, block.shape[dim] - width, None, axis...  9.38 us
    select_n x2, other arithmetic, per_device(): partner_tile = jnp.take(window, local_index.reshape(-1), axis=1)  8.77 us
    ppermute x1, waiting for transfers between devices, extended_2(): lax.ppermute(lax.slice_in_dim(block, 0, width, axis=dim), axis, backward)  7.55 us
  transfers between devices with their start and end apart: 4, of which 3 were waited for; matrix products, arithmetic and copies ran while one was open for 6% of the time, Pallas kernels for 0%

commit v1 on v0

v1 whole, which is shorter than its diff:
```python
import functools

import jax
import jax.numpy as jnp
from jax import lax
from jax.experimental import pallas as pl
from jax.experimental.pallas import tpu as pltpu
from jax.sharding import PartitionSpec as P

MESH = pl.DeviceIdType.MESH
OWN = 4
MAXOFF = 4
LOOK_AZ = 4
LOOK_RG = 16
EPS = 1e-06
STEP = 16
LANES = 256
PAD = 8
BLOCK = 8
IN_FLIGHT = 3

INNER = [(a, m) for a in range(4, 8) for m in range(1, 5) if a + m < 8]
CROSS = [(a, m) for a in (2, 3) for m in range(1, 5) if 4 <= a + m < 8]
CROSS += [(a, m) for a in range(4, 8) for m in range(1, 5) if a + m in (8, 9)]
FAR = [2, 3, 8, 9]


def slot(a, m):
    return 4 * a + m - 1


PLACE = {}
POWER = {}
for _edge in INNER:
    PLACE[_edge] = 2 * len(PLACE)
for _date in range(4, 8):
    POWER[_date] = 2 * len(INNER) + _date - 4
N_INNER = 2 * len(INNER) + 4
for _n, _edge in enumerate(CROSS):
    PLACE[_edge] = N_INNER + 2 * _n
for _n, _date in enumerate(FAR):
    POWER[_date] = N_INNER + 2 * len(CROSS) + _n
N_ALL = N_INNER + 2 * len(CROSS) + 4


def kernel(
    offsets, slc, interferogram, coherence,
    own, far, sel, sums, edge_sums, halo, results,
    own_sem, send_sem, recv_sem, halo_send, halo_recv, ship_send, ship_recv,
):
    rows = own.shape[2]
    cells = own.shape[3]
    steps = rows // STEP
    looks = rows // LOOK_AZ
    blocks = looks // BLOCK
    columns = cells // LOOK_RG
    d = lax.axis_index("date")
    s = lax.axis_index("strip")
    has = {
        "prev": d > 0,
        "next": d < lax.axis_size("date") - 1,
        "low": s > 0,
        "high": s < lax.axis_size("strip") - 1,
    }
    where = {
        "prev": {"date": d - 1},
        "next": {"date": d + 1},
        "low": {"strip": s - 1},
        "high": {"strip": s + 1},
    }
    order = [0, steps - 1] + list(range(1, steps - 1))

    def own_copy(step):
        part = (slice(None), slice(None), pl.ds(step * STEP, STEP))
        return pltpu.make_async_copy(slc.at[part], own.at[part], own_sem.at[step])

    def image_copy(side, step):
        n = 0 if side == "next" else 1
        first = 2 if side == "next" else 0
        return pltpu.make_async_remote_copy(
            src_ref=slc.at[:, pl.ds(first, 2), pl.ds(step * STEP, STEP)],
            dst_ref=far.at[n, :, :, pl.ds(step * STEP, STEP)],
            send_sem=send_sem.at[n, step],
            recv_sem=recv_sem.at[n, step],
            device_id=where[side],
            device_id_type=MESH,
        )

    def halo_copy(side):
        n = 0 if side == "high" else 1
        return pltpu.make_async_remote_copy(
            src_ref=edge_sums.at[n],
            dst_ref=halo.at[n],
            send_sem=halo_send.at[n],
            recv_sem=halo_recv.at[n],
            device_id=where[side],
            device_id_type=MESH,
        )

    def ship_copies(side, block):
        n, base, shift = (0, 16, -16) if side == "next" else (1, 8, 16)
        part = pl.ds(block * BLOCK, BLOCK)
        copies = []
        for i, (first, count) in enumerate(((3, 1), (6, 2))):
            copies.append(
                pltpu.make_async_remote_copy(
                    src_ref=results.at[pl.ds(base + first, count), :, part],
                    dst_ref=results.at[pl.ds(base + shift + first, count), :, part],
                    send_sem=ship_send.at[n, block, i],
                    recv_sem=ship_recv.at[n, block, i],
                    device_id=where[side],
                    device_id_type=MESH,
                )
            )
        return copies

    for step in order:
        own_copy(step).start()

    barrier = pltpu.get_barrier_semaphore()
    for side in has:
        @pl.when(has[side])
        def _(side=side):
            pl.semaphore_signal(barrier, inc=1, device_id=where[side], device_id_type=MESH)

    cell = lax.broadcasted_iota(jnp.int32, (cells, columns), 0)
    look = lax.broadcasted_iota(jnp.int32, (cells, columns), 1)
    sel[...] = jnp.where(cell // LOOK_RG == look, 1.0, 0.0).astype(jnp.bfloat16)

    pl.semaphore_wait(barrier, sum(h.astype(jnp.int32) for h in has.values()))

    def send(step):
        for side in ("next", "prev"):
            @pl.when(has[side])
            def _(side=side):
                image_copy(side, step).start()

    for step in order[:IN_FLIGHT]:
        send(step)

    for side, n in (("prev", 0), ("next", 1)):
        @pl.when(jnp.logical_not(has[side]))
        def _(n=n, side=side):
            far[n] = jnp.zeros(far.shape[1:], far.dtype)
            base = 3 if side == "prev" else 27
            results[base] = jnp.zeros(results.shape[1:], results.dtype)
            results[pl.ds(base + 3, 2)] = jnp.zeros((2,) + results.shape[1:], results.dtype)
    for side, n in (("low", 0), ("high", 1)):
        @pl.when(jnp.logical_not(has[side]))
        def _(n=n):
            halo[n] = jnp.zeros(halo.shape[1:], halo.dtype)

    def add_up(step, edges, dates, first, count):
        row = pl.ds(step * STEP, STEP)
        needed = sorted({a for a, m in edges} | {a + m for a, m in edges} | set(dates))

        def body(k, total):
            lane = pl.ds(pl.multiple_of(k * LANES, LANES), LANES)
            value = {}
            for a in needed:
                if 4 <= a < 8:
                    parts = [own[c, a - 4, row, lane] for c in range(2)]
                elif a < 4:
                    parts = [far[0, c, a - 2, row, lane] for c in range(2)]
                else:
                    parts = [far[1, c, a - 8, row, lane] for c in range(2)]
                value[a] = [p.astype(jnp.float32) for p in parts]
            terms = []
            for a, m in edges:
                (x, y), (u, v) = value[a], value[a + m]
                terms.append(x * u + y * v)
                terms.append(y * u - x * v)
            for a in dates:
                x, y = value[a]
                terms.append(x * x + y * y)
            packed = []
            for t in terms:
                high = t.astype(jnp.bfloat16)
                low = (t - high.astype(jnp.float32)).astype(jnp.bfloat16)
                packed.append(jnp.concatenate([high, low], axis=1))
            left = jnp.concatenate(packed, axis=0)
            weight = sel[lane, :]
            right = jnp.concatenate([weight, weight], axis=0)
            return total + jnp.dot(left, right, preferred_element_type=jnp.float32)

        total = lax.fori_loop(0, cells // LANES, body, jnp.zeros((count * STEP, columns), jnp.float32))
        sums[pl.ds(first, count), pl.ds(PAD + step * STEP, STEP), :] = total.reshape(count, STEP, columns)

    def windows(q, block):
        base = PAD + block * BLOCK * LOOK_AZ

        def every(shift):
            return sums[q, pl.ds(base + shift, BLOCK, stride=LOOK_AZ), :]

        inner = (every(0) + every(1)) + (every(2) + every(3))
        outer = (every(-2) + every(-1)) + (every(4) + every(5))
        return inner, inner + outer

    def finish(block, edges, power):
        for a, m in edges:
            for b in (a, a + m):
                if b not in power:
                    power[b] = windows(POWER[b], block)[1]
            look_re, win_re = windows(PLACE[a, m], block)
            look_im, win_im = windows(PLACE[a, m] + 1, block)
            size = jnp.sqrt(win_re * win_re + win_im * win_im)
            part = pl.ds(block * BLOCK, BLOCK)
            results[slot(a, m), 0, part] = look_re * (1.0 / (LOOK_AZ * LOOK_RG))
            results[slot(a, m), 1, part] = look_im * (1.0 / (LOOK_AZ * LOOK_RG))
            results[slot(a, m), 2, part] = size / jnp.sqrt(power[a] * power[a + m] + EPS)

    for step in order:
        own_copy(step).wait()
        add_up(step, INNER, list(range(4, 8)), 0, N_INNER)

    shipped = [(4, 4), (5, 3), (5, 4), (2, 4), (3, 3), (3, 4)]
    kept = INNER + [e for e in CROSS if e not in shipped]

    def finish_block(block):
        power = {}
        finish(block, shipped, power)
        for side in ("next", "prev"):
            @pl.when(has[side])
            def _(side=side):
                for copy in ship_copies(side, block):
                    copy.start()
        finish(block, kept, power)

    ready = set()
    finished = set()
    for n, step in enumerate(order):
        for side in ("prev", "next"):
            @pl.when(has[side])
            def _(side=side):
                image_copy("next" if side == "prev" else "prev", step).wait_recv()
        if n + IN_FLIGHT < steps:
            send(order[n + IN_FLIGHT])
        add_up(step, CROSS, FAR, N_INNER, N_ALL - N_INNER)
        ready.add(step)
        if n == 1:
            for q in range(N_ALL):
                edge_sums[0, pl.ds(q, 1)] = sums[q, pl.ds(PAD + rows - 2, 1)] + sums[q, pl.ds(PAD + rows - 1, 1)]
                edge_sums[1, pl.ds(q, 1)] = sums[q, pl.ds(PAD, 1)] + sums[q, pl.ds(PAD + 1, 1)]
            for side in ("high", "low"):
                @pl.when(has[side])
                def _(side=side):
                    halo_copy(side).start()
        if n == 2:
            for side, opposite in (("low", "high"), ("high", "low")):
                @pl.when(has[side])
                def _(opposite=opposite):
                    halo_copy(opposite).wait_recv()
            zero = jnp.zeros((1, columns), jnp.float32)
            for q in range(N_ALL):
                sums[q, pl.ds(PAD - 2, 1)] = zero
                sums[q, pl.ds(PAD - 1, 1)] = halo[0, pl.ds(q, 1)]
                sums[q, pl.ds(PAD + rows, 1)] = halo[1, pl.ds(q, 1)]
                sums[q, pl.ds(PAD + rows + 1, 1)] = zero
        if n >= 2:
            per = BLOCK * LOOK_AZ // STEP
            for block in range(blocks):
                touched = {p for p in range(block * per - 1, block * per + per + 1) if 0 <= p < steps}
                if block not in finished and touched <= ready:
                    finish_block(block)
                    finished.add(block)

    for side, opposite in (("next", "prev"), ("prev", "next")):
        @pl.when(has[side])
        def _(side=side, opposite=opposite):
            for block in range(blocks):
                for copy in ship_copies(opposite, block):
                    copy.wait_recv()

    for i in range(OWN):
        for k in range(4):
            offset = offsets[i, k]
            place = 4 * (OWN + i + jnp.minimum(offset, 0)) + jnp.abs(offset) - 1
            sign = jnp.where(offset > 0, 1.0, -1.0)
            chosen = results[place]
            interferogram[i, k, 0] = chosen[0]
            interferogram[i, k, 1] = chosen[1] * sign
            coherence[i, k] = chosen[2]

    for side in ("next", "prev"):
        @pl.when(has[side])
        def _(side=side):
            for step in order:
                image_copy(side, step).wait_send()
            for block in range(blocks):
                for copy in ship_copies(side, block):
                    copy.wait_send()
    for side in ("high", "low"):
        @pl.when(has[side])
        def _(side=side):
            halo_copy(side).wait_send()


def per_device(slc, partner_offset):
    _, dates, rows, cells = slc.shape
    columns = cells // LOOK_RG
    looks = rows // LOOK_AZ
    steps = rows // STEP
    blocks = looks // BLOCK
    f32 = jnp.float32
    return pl.pallas_call(
        kernel,
        out_shape=(
            jax.ShapeDtypeStruct((dates, 4, 2, looks, columns), f32),
            jax.ShapeDtypeStruct((dates, 4, looks, columns), f32),
        ),
        in_specs=[
            pl.BlockSpec(memory_space=pltpu.SMEM),
            pl.BlockSpec(memory_space=pl.ANY),
        ],
        out_specs=[pl.BlockSpec(memory_space=pltpu.VMEM)] * 2,
        scratch_shapes=[
            pltpu.VMEM((2, dates, rows, cells), slc.dtype),
            pltpu.VMEM((2, 2, 2, rows, cells), slc.dtype),
            pltpu.VMEM((cells, columns), jnp.bfloat16),
            pltpu.VMEM((N_ALL, rows + 2 * PAD, columns), f32),
            pltpu.VMEM((2, N_ALL, columns), f32),
            pltpu.VMEM((2, N_ALL, columns), f32),
            pltpu.VMEM((32, 3, looks, columns), f32),
            pltpu.SemaphoreType.DMA((steps,)),
            pltpu.SemaphoreType.DMA((2, steps)),
            pltpu.SemaphoreType.DMA((2, steps)),
            pltpu.SemaphoreType.DMA((2,)),
            pltpu.SemaphoreType.DMA((2,)),
            pltpu.SemaphoreType.DMA((2, blocks, 2)),
            pltpu.SemaphoreType.DMA((2, blocks, 2)),
        ],
        compiler_params=pltpu.CompilerParams(
            collective_id=0, has_side_effects=True, vmem_limit_bytes=48 * 1024 * 1024
        ),
    )(partner_offset, slc)


def solution(mesh):
    return jax.shard_map(
        per_device,
        mesh=mesh,
        in_specs=(P(None, "date", "strip", None), P("date", None)),
        out_specs=(P("date", None, None, "strip", None), P("date", None, "strip", None)),
        check_vma=False,
    )
```

time: 219 us -> 74.1 us (0.34)
  the two profiles are of different devices: /device:TPU:5 before, /device:TPU:61 now
where the time goes in v1:
time: 74.1 us; the launch traced here: 73.9 us
  Pallas kernels  68.9 us (93%)
  local copies, waits for them, and re-layouts  4.36 us (6%)
    pallas_call x1, Pallas kernels, per_device(): pl.pallas_call(kernel, out_shape=(jax.ShapeDtypeStruct((dates, 4, 2, look...  68.9 us
    unnamed x6, local copies, waits for them, and re-layouts  4.36 us

profile of v1, /device:TPU:61, one launch (start us, length us, event | category | flops | bytes accessed | tf_op | source)
XLA Modules:
  0.0 73.9 jit_solution(2241526898224646640)
XLA Ops:
  0.6 0.0 copy-start
  0.6 2.2 %copy-done = bf16[2,4,128,2048]{3,2,1,0:T(8,128)(2,1)S(1)} copy-done((bf16[2,4,128,2048]{3,2,1,0:T(8,128)(2,1)S(1)}, bf16[2,4,128,2048]{3,2,1,0:T(8,128)(2,1)}, u32[]{:S(2)}) %copy-start) | copy-done | bytes 4194328
  2.8 0.0 copy-start.1
  2.8 0.7 copy-done.1
  3.5 68.9 %shard_map.41 = (f32[4,4,2,32,128]{4,3,2,1,0:T(8,128)S(1)}, f32[4,4,32,128]{3,2,1,0:T(8,128)S(1)}) custom-call(s32[4,4]{1,0:T(4,128)S(1)} %copy-done.1, bf16[2,4,128,2048]{3,2,1,0:T(8,128)(2,1)S(1)} %copy-done), custom_call_target="tpu_custom_call" | custom-call | tf_op jit(solution)/shard_map/pallas_call | solution.py:305
  72.4 0.8 %copy.6 = f32[4,4,2,32,128]{4,3,2,1,0:T(8,128)} copy(f32[4,4,2,32,128]{4,3,2,1,0:T(8,128)S(1)} %get-tuple-element.4) | data formatting | bytes 1048576
  73.2 0.7 copy.7
Async XLA Ops:
  0.6 2.2 %copy-start = (bf16[2,4,128,2048]{3,2,1,0:T(8,128)(2,1)S(1)}, bf16[2,4,128,2048]{3,2,1,0:T(8,128)(2,1)}, u32[]{:S(2)}) copy-start(bf16[2,4,128,2048]{3,2,1,0:T(8,128)(2,1)} %slc.1) | copy-start | bytes 12582916
  2.8 0.7 copy-start.1

commit v2 on v1

v2 whole, which is shorter than its diff:
```python
import functools

import jax
import jax.numpy as jnp
from jax import lax
from jax.experimental import pallas as pl
from jax.experimental.pallas import tpu as pltpu
from jax.sharding import PartitionSpec as P

MESH = pl.DeviceIdType.MESH
OWN = 4
MAXOFF = 4
LOOK_AZ = 4
LOOK_RG = 16
EPS = 1e-06
LANES = 1024
INNER_ROWS = 32
PAD = 8
BLOCK = 8
IN_FLIGHT = 3
BOTH, NEAR, OTHER = (0, 2), (0, 1), (1, 2)
UNITS = [(0, 16, BOTH), (112, 16, BOTH)]
UNITS += [(16, 32, NEAR), (48, 32, NEAR), (80, 32, NEAR)]
UNITS += [(80, 32, OTHER), (48, 32, OTHER), (32, 16, OTHER), (16, 16, OTHER)]
EDGES_AT = 1
RELAY_AT = (2, 4)
HALO_AT = 7

INNER = [(a, m) for a in range(4, 8) for m in range(1, 5) if a + m < 8]
CROSS = {
    NEAR: [(3, m) for m in range(1, 5)] + [(a, 8 - a) for a in range(4, 8)],
    OTHER: [(2, m) for m in range(2, 5)] + [(a, 9 - a) for a in range(5, 8)],
}
FAR = {NEAR: [3, 8], OTHER: [2, 9]}


def slot(a, m):
    return 4 * a + m - 1


PLACE = {}
POWER = {}
SPAN = {}


def give_places(name, edges, dates):
    first = 2 * len(PLACE) + len(POWER)
    for edge in edges:
        PLACE[edge] = 2 * len(PLACE) + len(POWER)
    for date in dates:
        POWER[date] = 2 * len(PLACE) + len(POWER)
    SPAN[name] = (first, 2 * len(PLACE) + len(POWER) - first)


give_places("inner", INNER, [4, 5, 6, 7])
give_places(NEAR, CROSS[NEAR], FAR[NEAR])
give_places(OTHER, CROSS[OTHER], FAR[OTHER])
N_ALL = SPAN[OTHER][0] + SPAN[OTHER][1]
SHIPPED = {"next": [(4, 4), (5, 3), (5, 4)], "prev": [(3, 3), (3, 4), (2, 4)]}


def kernel(
    offsets, slc, interferogram, coherence,
    own, far, own_wide, far_wide, sel, sums, edge_sums, halo, relayed, results,
    own_sem, send_sem, recv_sem, halo_send, halo_recv, relay_send, relay_recv, ship_send, ship_recv,
):
    rows = own.shape[2]
    cells = own.shape[3]
    looks = rows // LOOK_AZ
    blocks = looks // BLOCK
    columns = cells // LOOK_RG
    d = lax.axis_index("date")
    s = lax.axis_index("strip")
    has = {
        "prev": d > 0,
        "next": d < lax.axis_size("date") - 1,
        "low": s > 0,
        "high": s < lax.axis_size("strip") - 1,
    }
    where = {
        "prev": {"date": d - 1},
        "next": {"date": d + 1},
        "low": {"strip": s - 1},
        "high": {"strip": s + 1},
    }
    place = d % 4
    inner = (place == 1) | (place == 2)
    remote = {"high": s % 2 == 1, "low": s % 2 == 0}
    greets = {
        "prev": has["prev"],
        "next": has["next"],
        "low": has["low"] & (inner | jnp.logical_not(remote["low"])),
        "high": has["high"] & (inner | jnp.logical_not(remote["high"])),
    }
    false = d < 0
    later = {"prev": false, "next": false, "low": false, "high": remote["high"]}
    former = {"prev": false, "next": false, "low": remote["low"], "high": false}

    def own_copy(step):
        part = (slice(None), slice(None), pl.ds(step * INNER_ROWS, INNER_ROWS))
        return pltpu.make_async_copy(slc.at[part], own.at[part], own_sem.at[step])

    def image_copy(side, unit):
        first, height, (low, high) = UNITS[unit]
        n = 0 if side == "next" else 1
        row = pl.ds(first, height)
        date = pl.ds(4 - high, high - low) if side == "next" else pl.ds(low, high - low)
        slots = pl.ds(2 - high, high - low) if side == "next" else pl.ds(low, high - low)
        return pltpu.make_async_remote_copy(
            src_ref=slc.at[:, date, row],
            dst_ref=far.at[n, :, slots, row],
            send_sem=send_sem.at[n, unit],
            recv_sem=recv_sem.at[n, unit],
            device_id=where[side],
            device_id_type=MESH,
        )

    def halo_copy(n, source, side, send, target=None, recv=None):
        return pltpu.make_async_remote_copy(
            src_ref=source,
            dst_ref=halo.at[n] if target is None else target,
            send_sem=send,
            recv_sem=halo_recv.at[n] if recv is None else recv,
            device_id=where[side],
            device_id_type=MESH,
        )

    def ship_copy(side, edge, block):
        a, m = edge
        n, shift = (0, -16) if side == "next" else (1, 16)
        i = SHIPPED[side].index(edge)
        part = pl.ds(block * BLOCK, BLOCK)
        return pltpu.make_async_remote_copy(
            src_ref=results.at[slot(a, m), :, part],
            dst_ref=results.at[slot(a, m) + shift, :, part],
            send_sem=ship_send.at[n, i, block],
            recv_sem=ship_recv.at[n, i, block],
            device_id=where[side],
            device_id_type=MESH,
        )

    for step in range(rows // INNER_ROWS):
        own_copy(step).start()

    barrier = pltpu.get_barrier_semaphore()

    def count(flags):
        return sum(flag.astype(jnp.int32) for flag in flags)

    for side in has:
        @pl.when(greets[side] & jnp.logical_not(later[side] | former[side]))
        def _(side=side):
            pl.semaphore_signal(barrier, inc=1, device_id=where[side], device_id_type=MESH)

    look = lax.broadcasted_iota(jnp.int32, (128, columns), 1)
    cell = lax.broadcasted_iota(jnp.int32, (128, columns), 0)
    for tile in range(cells // 128):
        ones = jnp.where((cell + tile * 128) // LOOK_RG == look, 1.0, 0.0).astype(jnp.bfloat16)
        sel[tile, pl.ds(0, 128)] = ones
        sel[tile, pl.ds(128, 128)] = ones

    pl.semaphore_wait(barrier, count(greets[side] & jnp.logical_not(later[side]) for side in has))
    for side in has:
        @pl.when(greets[side] & (later[side] | former[side]))
        def _(side=side):
            pl.semaphore_signal(barrier, inc=1, device_id=where[side], device_id_type=MESH)

    def send(unit):
        for side in ("next", "prev"):
            @pl.when(has[side])
            def _(side=side):
                image_copy(side, unit).start()

    for unit in range(IN_FLIGHT):
        send(unit)

    for side, n in (("prev", 0), ("next", 1)):
        @pl.when(jnp.logical_not(has[side]))
        def _(n=n, side=side):
            far[n] = jnp.zeros(far.shape[1:], far.dtype)
            base = 3 if side == "prev" else 27
            results[base] = jnp.zeros(results.shape[1:], results.dtype)
            results[pl.ds(base + 3, 2)] = jnp.zeros((2,) + results.shape[1:], results.dtype)
    for side, n in (("low", 0), ("high", 1)):
        @pl.when(jnp.logical_not(has[side]))
        def _(n=n):
            halo[n] = jnp.zeros(halo.shape[1:], halo.dtype)

    def widen(source, target, row):
        def body(k, carry):
            lane = pl.ds(pl.multiple_of(k * 128, 128), 128)
            target[:, :, k] = source[:, :, row, lane].astype(jnp.float32)
            return carry

        lax.fori_loop(0, cells // 128, body, 0, unroll=2)

    def add_up(base, far_base, height, edges, dates, first, count):
        pairs = height // 2
        groups = edges if dates is None else [(edges, dates)]
        every = [e for pairs_of, _ in groups for e in pairs_of]
        needed = sorted({a for a, m in every} | {a + m for a, m in every})

        def body(k, total):
            packed = []
            weights = []
            for part in range(LANES // 128):
                tile = k * (LANES // 128) + part
                value = {}
                for a in needed:
                    value[a] = []
                    for c in range(2):
                        for odd in range(2):
                            row = pl.ds((base if 4 <= a < 8 else far_base) + odd, pairs, stride=2)
                            if 4 <= a < 8:
                                value[a].append(own_wide[c, a - 4, tile, row])
                            elif a < 4:
                                value[a].append(far_wide[0, c, a - 2, tile, row])
                            else:
                                value[a].append(far_wide[1, c, a - 8, tile, row])
                terms = []
                for pairs_of, alone in groups:
                    for a, m in pairs_of:
                        (x, z, y, w), (u, p, v, q) = value[a], value[a + m]
                        terms.append((x * u + y * v) + (z * p + w * q))
                        terms.append((y * u - x * v) + (w * p - z * q))
                    for a in alone:
                        x, z, y, w = value[a]
                        terms.append((x * x + y * y) + (z * z + w * w))
                left = jnp.concatenate(terms, axis=0)
                high = left.astype(jnp.bfloat16)
                low = (left - high.astype(jnp.float32)).astype(jnp.bfloat16)
                packed += [high, low]
                weights.append(sel[tile])
            left = jnp.concatenate(packed, axis=1)
            right = jnp.concatenate(weights, axis=0)
            return total + jnp.dot(left, right, preferred_element_type=jnp.float32)

        total = lax.fori_loop(0, cells // LANES, body, jnp.zeros((count * pairs, columns), jnp.float32))
        sums[pl.ds(first, count), pl.ds(PAD + base // 2, pairs), :] = total.reshape(count, pairs, columns)

    def windows(q, block):
        base = PAD + block * BLOCK * 2

        def every(shift):
            return sums[q, pl.ds(base + shift, BLOCK, stride=2), :]

        inner = every(0) + every(1)
        return inner, inner + (every(-1) + every(2))

    def finish(block, edges, power):
        for a, m in edges:
            for b in (a, a + m):
                if b not in power:
                    power[b] = windows(POWER[b], block)[1]
            look_re, win_re = windows(PLACE[a, m], block)
            look_im, win_im = windows(PLACE[a, m] + 1, block)
            size = jnp.sqrt(win_re * win_re + win_im * win_im)
            part = pl.ds(block * BLOCK, BLOCK)
            results[slot(a, m), 0, part] = look_re * (1.0 / (LOOK_AZ * LOOK_RG))
            results[slot(a, m), 1, part] = look_im * (1.0 / (LOOK_AZ * LOOK_RG))
            results[slot(a, m), 2, part] = size / jnp.sqrt(power[a] * power[a + m] + EPS)

    for step in range(rows // INNER_ROWS):
        own_copy(step).wait()
        row = pl.ds(step * INNER_ROWS, INNER_ROWS)
        widen(own, own_wide.at[:, :, :, row], row)
        add_up(step * INNER_ROWS, 0, INNER_ROWS, INNER, [4, 5, 6, 7], *SPAN["inner"])

    @pl.when(greets["high"] & later["high"])
    def _():
        pl.semaphore_wait(barrier, 1)

    def on_strip(which, body):
        for side, n in (("high", 0), ("low", 1)):
            @pl.when(has[side] & remote[side] & which)
            def _(side=side, n=n):
                body(side, n)

    def send_edges():
        for q in range(N_ALL):
            edge_sums[0, pl.ds(q, 1)] = sums[q, pl.ds(PAD + rows // 2 - 1, 1)]
            edge_sums[1, pl.ds(q, 1)] = sums[q, pl.ds(PAD, 1)]
        for side, n in (("high", 0), ("low", 1)):
            @pl.when(has[side] & jnp.logical_not(remote[side]))
            def _(side=side, n=n):
                halo_copy(n, edge_sums.at[n], side, halo_send.at[n]).start()
        on_strip(inner, lambda side, n: halo_copy(n, edge_sums.at[n], side, halo_send.at[n]).start())
        for at, toward in ((0, "next"), (3, "prev")):
            on_strip(place == at, lambda side, n, toward=toward: relay_out(n, toward).start())

    def relay_out(n, toward):
        return halo_copy(n, edge_sums.at[n], toward, relay_send.at[0], relayed.at[0], relay_recv.at[0])

    def relay_over(side, n):
        return halo_copy(n, relayed.at[0], side, relay_send.at[1], relayed.at[1], relay_recv.at[1])

    def relay_back(n, toward):
        return halo_copy(1 - n, relayed.at[1], toward, relay_send.at[2])

    def pass_over(side, n):
        relay_out(n, "next").wait_recv()
        relay_over(side, n).start()

    def pass_back():
        for at, toward in ((1, "prev"), (2, "next")):
            def body(side, n, toward=toward):
                relay_over(side, n).wait_recv()
                relay_back(n, toward).start()
            on_strip(place == at, body)

    def take_halo():
        for side, opposite, n in (("low", "high", 0), ("high", "low", 1)):
            @pl.when(has[side])
            def _(opposite=opposite, n=n):
                halo_copy(n, edge_sums.at[n], opposite, halo_send.at[n]).wait_recv()
        for q in range(N_ALL):
            sums[q, pl.ds(PAD - 1, 1)] = halo[0, pl.ds(q, 1)]
            sums[q, pl.ds(PAD + rows // 2, 1)] = halo[1, pl.ds(q, 1)]

    def finish_block(name, block):
        edges = INNER if name == "inner" else CROSS[name]
        power = {}
        for side in ("next", "prev"):
            owed = [e for e in edges if e in SHIPPED[side]]
            finish(block, owed, power)
            if owed:
                @pl.when(has[side])
                def _(side=side, owed=owed):
                    for edge in owed:
                        ship_copy(side, edge, block).start()
        finish(block, [e for e in edges if e not in SHIPPED["next"] + SHIPPED["prev"]], power)

    ready = {"inner": set(range(rows)), NEAR: set(), OTHER: set()}
    finished = set()
    for unit, (first, height, dates) in enumerate(UNITS):
        for side in ("prev", "next"):
            @pl.when(has[side])
            def _(side=side):
                image_copy("next" if side == "prev" else "prev", unit).wait_recv()
        if unit + IN_FLIGHT < len(UNITS):
            send(unit + IN_FLIGHT)
        if unit == HALO_AT:
            take_halo()
        row = pl.ds(first, height)
        for side, (low, high) in ((0, (2 - dates[1], 2 - dates[0])), (1, dates)):
            date = pl.ds(low, high - low)
            widen(far.at[side, :, date], far_wide.at[side, :, date, :, pl.ds(0, height)], row)
        names = [name for name in (NEAR, OTHER) if dates[0] <= name[0] and name[1] <= dates[1]]
        begin = SPAN[names[0]][0]
        number = sum(SPAN[name][1] for name in names)
        edges = [(CROSS[name], FAR[name]) for name in names]
        add_up(first, 0, height, edges, None, begin, number)
        for name in names:
            ready[name] |= set(range(first, first + height))
        if unit == EDGES_AT:
            send_edges()
        if unit == RELAY_AT[0]:
            on_strip(inner, pass_over)
        if unit == RELAY_AT[1]:
            pass_back()
        if unit > EDGES_AT:
            for name in (NEAR, OTHER, "inner"):
                for block in range(blocks):
                    height_of = BLOCK * LOOK_AZ
                    reach = set(range(max(block * height_of - 2, 0), min((block + 1) * height_of + 2, rows)))
                    inside = 0 < block < blocks - 1
                    if (name, block) not in finished and reach <= ready[name] and (inside or unit >= HALO_AT):
                        finish_block(name, block)
                        finished.add((name, block))

    for side, opposite in (("next", "prev"), ("prev", "next")):
        @pl.when(has[side])
        def _(side=side, opposite=opposite):
            for block in range(blocks):
                for edge in SHIPPED[opposite]:
                    ship_copy(opposite, edge, block).wait_recv()

    for i in range(OWN):
        for k in range(4):
            offset = offsets[i, k]
            place = 4 * (OWN + i + jnp.minimum(offset, 0)) + jnp.abs(offset) - 1
            sign = jnp.where(offset > 0, 1.0, -1.0)
            chosen = results[place]
            interferogram[i, k, 0] = chosen[0]
            interferogram[i, k, 1] = chosen[1] * sign
            coherence[i, k] = chosen[2]

    for side in ("next", "prev"):
        @pl.when(has[side])
        def _(side=side):
            for unit in range(len(UNITS)):
                image_copy(side, unit).wait_send()
            for block in range(blocks):
                for edge in SHIPPED[side]:
                    ship_copy(side, edge, block).wait_send()
    for side, n in (("high", 0), ("low", 1)):
        @pl.when(has[side] & (inner | jnp.logical_not(remote[side])))
        def _(side=side, n=n):
            halo_copy(n, edge_sums.at[n], side, halo_send.at[n]).wait_send()
    on_strip(jnp.logical_not(inner), lambda side, n: relay_out(n, "next").wait_send())
    on_strip(inner, lambda side, n: relay_over(side, n).wait_send())
    on_strip(inner, lambda side, n: relay_back(n, "next").wait_send())


def per_device(slc, partner_offset):
    _, dates, rows, cells = slc.shape
    columns = cells // LOOK_RG
    looks = rows // LOOK_AZ
    steps = rows // INNER_ROWS
    blocks = looks // BLOCK
    f32 = jnp.float32
    return pl.pallas_call(
        kernel,
        out_shape=(
            jax.ShapeDtypeStruct((dates, 4, 2, looks, columns), f32),
            jax.ShapeDtypeStruct((dates, 4, looks, columns), f32),
        ),
        in_specs=[
            pl.BlockSpec(memory_space=pltpu.SMEM),
            pl.BlockSpec(memory_space=pl.ANY),
        ],
        out_specs=[pl.BlockSpec(memory_space=pltpu.VMEM)] * 2,
        scratch_shapes=[
            pltpu.VMEM((2, dates, rows, cells), slc.dtype),
            pltpu.VMEM((2, 2, 2, rows, cells), slc.dtype),
            pltpu.VMEM((2, dates, cells // 128, rows, 128), f32),
            pltpu.VMEM((2, 2, 2, cells // 128, INNER_ROWS, 128), f32),
            pltpu.VMEM((cells // 128, 256, columns), jnp.bfloat16),
            pltpu.VMEM((N_ALL, rows // 2 + 2 * PAD, columns), f32),
            pltpu.VMEM((2, N_ALL, columns), f32),
            pltpu.VMEM((2, N_ALL, columns), f32),
            pltpu.VMEM((2, N_ALL, columns), f32),
            pltpu.VMEM((32, 3, looks, columns), f32),
            pltpu.SemaphoreType.DMA((steps,)),
            pltpu.SemaphoreType.DMA((2, len(UNITS))),
            pltpu.SemaphoreType.DMA((2, len(UNITS))),
            pltpu.SemaphoreType.DMA((2,)),
            pltpu.SemaphoreType.DMA((2,)),
            pltpu.SemaphoreType.DMA((3,)),
            pltpu.SemaphoreType.DMA((2,)),
            pltpu.SemaphoreType.DMA((2, 3, blocks)),
            pltpu.SemaphoreType.DMA((2, 3, blocks)),
        ],
        compiler_params=pltpu.CompilerParams(
            collective_id=0, has_side_effects=True, vmem_limit_bytes=59 * 1024 * 1024
        ),
    )(partner_offset, slc)


def solution(mesh):
    return jax.shard_map(
        per_device,
        mesh=mesh,
        in_specs=(P(None, "date", "strip", None), P("date", None)),
        out_specs=(P("date", None, None, "strip", None), P("date", None, "strip", None)),
        check_vma=False,
    )
```

time: 74.1 us -> 71.3 us (0.962)
  the two profiles are of different devices: /device:TPU:61 before, /device:TPU:6 now
where the time goes in v2:
time: 71.3 us; the launch traced here: 71.1 us
  Pallas kernels  66.9 us (94%)
  local copies, waits for them, and re-layouts  3.55 us (5%)
    pallas_call x1, Pallas kernels, per_device(): pl.pallas_call(kernel, out_shape=(jax.ShapeDtypeStruct((dates, 4, 2, look...  66.9 us
    unnamed x2, local copies, waits for them, and re-layouts  3.55 us

profile of v2, /device:TPU:6, one launch (start us, length us, event | category | flops | bytes accessed | tf_op | source)
XLA Modules:
  0.0 71.1 jit_solution(12269103633827776765)
XLA Ops:
  0.6 66.9 %shard_map.41 = (f32[4,4,2,32,128]{4,3,2,1,0:T(8,128)}, f32[4,4,32,128]{3,2,1,0:T(8,128)}) custom-call(s32[4,4]{1,0:T(4,128)} %offsets.1, bf16[2,4,128,2048]{3,2,1,0:T(8,128)(2,1)} %slc.1), custom_call_target="tpu_custom_call" | custom-call | tf_op jit(solution)/shard_map/pallas_call | solution.py:412
  67.5 1.9 %copy.6 = f32[4,4,2,32,128]{4,3,2,1,0:T(8,128)} copy(f32[4,4,2,32,128]{4,3,2,1,0:T(8,128)} %get-tuple-element.4) | data formatting | bytes 1048576
  69.4 1.7 %copy.7 = f32[4,4,32,128]{3,2,1,0:T(8,128)} copy(f32[4,4,32,128]{3,2,1,0:T(8,128)} %get-tuple-element.5) | data formatting | bytes 524288

commit v3 on v2

--- a/solution.py
+++ b/solution.py
@@ -24,6 +24,7 @@
 UNITS += [(80, 32, OTHER), (48, 32, OTHER), (32, 16, OTHER), (16, 16, OTHER)]
 EDGES_AT = 1
 RELAY_AT = (2, 4)
+SHIP_AT = 6
 HALO_AT = 7
 
 INNER = [(a, m) for a in range(4, 8) for m in range(1, 5) if a + m < 8]
@@ -60,9 +61,9 @@
 
 
 def kernel(
-    offsets, slc, interferogram, coherence,
-    own, far, own_wide, far_wide, sel, sums, edge_sums, halo, relayed, results,
-    own_sem, send_sem, recv_sem, halo_send, halo_recv, relay_send, relay_recv, ship_send, ship_recv,
+    partner_offset, slc, interferogram, coherence,
+    offsets, own, far, own_wide, far_wide, sel, sums, edge_sums, halo, relayed, results,
+    offset_sem, own_sem, send_sem, recv_sem, halo_send, halo_recv, relay_send, relay_recv, ship_send, ship_recv,
 ):
     rows = own.shape[2]
     cells = own.shape[3]
@@ -139,8 +140,10 @@
             device_id_type=MESH,
         )
 
+    offset_copy = pltpu.make_async_copy(partner_offset, offsets, offset_sem)
     for step in range(rows // INNER_ROWS):
         own_copy(step).start()
+    offset_copy.start()
 
     barrier = pltpu.get_barrier_semaphore()
 
@@ -364,7 +367,8 @@
                     height_of = BLOCK * LOOK_AZ
                     reach = set(range(max(block * height_of - 2, 0), min((block + 1) * height_of + 2, rows)))
                     inside = 0 < block < blocks - 1
-                    if (name, block) not in finished and reach <= ready[name] and (inside or unit >= HALO_AT):
+                    late = (0 if name == "inner" else SHIP_AT) if inside else HALO_AT
+                    if (name, block) not in finished and reach <= ready[name] and unit >= late:
                         finish_block(name, block)
                         finished.add((name, block))
 
@@ -375,6 +379,7 @@
                 for edge in SHIPPED[opposite]:
                     ship_copy(opposite, edge, block).wait_recv()
 
+    offset_copy.wait()
     for i in range(OWN):
         for k in range(4):
             offset = offsets[i, k]
@@ -416,11 +421,12 @@
             jax.ShapeDtypeStruct((dates, 4, looks, columns), f32),
         ),
         in_specs=[
-            pl.BlockSpec(memory_space=pltpu.SMEM),
-            pl.BlockSpec(memory_space=pl.ANY),
+            pl.BlockSpec(memory_space=pltpu.HBM),
+            pl.BlockSpec(memory_space=pltpu.HBM),
         ],
         out_specs=[pl.BlockSpec(memory_space=pltpu.VMEM)] * 2,
         scratch_shapes=[
+            pltpu.SMEM(partner_offset.shape, partner_offset.dtype),
             pltpu.VMEM((2, dates, rows, cells), slc.dtype),
             pltpu.VMEM((2, 2, 2, rows, cells), slc.dtype),
             pltpu.VMEM((2, dates, cells // 128, rows, 128), f32),
@@ -431,6 +437,7 @@
             pltpu.VMEM((2, N_ALL, columns), f32),
             pltpu.VMEM((2, N_ALL, columns), f32),
             pltpu.VMEM((32, 3, looks, columns), f32),
+            pltpu.SemaphoreType.DMA,
             pltpu.SemaphoreType.DMA((steps,)),
             pltpu.SemaphoreType.DMA((2, len(UNITS))),
             pltpu.SemaphoreType.DMA((2, len(UNITS))),
@@ -442,7 +449,7 @@
             pltpu.SemaphoreType.DMA((2, 3, blocks)),
         ],
         compiler_params=pltpu.CompilerParams(
-            collective_id=0, has_side_effects=True, vmem_limit_bytes=59 * 1024 * 1024
+            collective_id=0, has_side_effects=True, vmem_limit_bytes=211 * 1024 * 256
         ),
     )(partner_offset, slc)
 

time: 71.3 us -> 67.4 us (0.945)
  Pallas kernels: 66.9 us -> 64.5 us
  local copies, waits for them, and re-layouts: 3.55 us -> 2.17 us
    pallas_call x1, Pallas kernels: 66.9 us -> 64.5 us  [per_device(): pl.pallas_call(kernel, out_shape=(jax.ShapeDtypeStruct((dates, 4, 2, look...]
    unnamed x2 -> x4, local copies, waits for them, and re-layouts: 3.55 us -> 2.17 us
where the time goes in v3:
time: 67.4 us; the launch traced here: 67.3 us
  Pallas kernels  64.5 us (96%)
  local copies, waits for them, and re-layouts  2.17 us (3%)
    pallas_call x1, Pallas kernels, per_device(): pl.pallas_call(kernel, out_shape=(jax.ShapeDtypeStruct((dates, 4, 2, look...  64.5 us
    unnamed x4, local copies, waits for them, and re-layouts  2.17 us

profile of v3, /device:TPU:6, one launch (start us, length us, event | category | flops | bytes accessed | tf_op | source)
XLA Modules:
  0.0 67.3 jit_solution(8411339635073778121)
XLA Ops:
  0.6 0.0 copy-start
  0.6 0.7 copy-done
  1.3 64.5 %shard_map.41 = (f32[4,4,2,32,128]{4,3,2,1,0:T(8,128)S(1)}, f32[4,4,32,128]{3,2,1,0:T(8,128)S(1)}) custom-call(s32[4,4]{1,0:T(4,128)S(1)} %copy-done, bf16[2,4,128,2048]{3,2,1,0:T(8,128)(2,1)} %slc.1), custom_call_target="tpu_custom_call" | custom-call | tf_op jit(solution)/shard_map/pallas_call | solution.py:417
  65.8 0.8 %copy.6 = f32[4,4,2,32,128]{4,3,2,1,0:T(8,128)} copy(f32[4,4,2,32,128]{4,3,2,1,0:T(8,128)S(1)} %get-tuple-element.4) | data formatting | bytes 1048576
  66.6 0.7 %copy.7 = f32[4,4,32,128]{3,2,1,0:T(8,128)} copy(f32[4,4,32,128]{3,2,1,0:T(8,128)S(1)} %get-tuple-element.5) | data formatting | bytes 524288
Async XLA Ops:
  0.6 0.7 %copy-start = (s32[4,4]{1,0:T(4,128)S(1)}, s32[4,4]{1,0:T(4,128)}, u32[]{:S(2)}) copy-start(s32[4,4]{1,0:T(4,128)} %partner_offset.1) | copy-start | bytes 196

commit v4 on v3

--- a/solution.py
+++ b/solution.py
@@ -21,18 +21,24 @@
 BOTH, NEAR, OTHER = (0, 2), (0, 1), (1, 2)
 UNITS = [(0, 16, BOTH), (112, 16, BOTH)]
 UNITS += [(16, 32, NEAR), (48, 32, NEAR), (80, 32, NEAR)]
-UNITS += [(80, 32, OTHER), (48, 32, OTHER), (32, 16, OTHER), (16, 16, OTHER)]
+UNITS += [(80, 16, OTHER), (96, 16, OTHER), (48, 32, OTHER), (32, 16, OTHER), (16, 16, OTHER)]
+LAST = len(UNITS) - 1
 EDGES_AT = 1
 RELAY_AT = (2, 4)
-SHIP_AT = 6
-HALO_AT = 7
+SHIFT = 5
+BORROW_AT = 7
+SHIP_AT = 7
+HALO_AT = 8
 
 INNER = [(a, m) for a in range(4, 8) for m in range(1, 5) if a + m < 8]
-CROSS = {
-    NEAR: [(3, m) for m in range(1, 5)] + [(a, 8 - a) for a in range(4, 8)],
-    OTHER: [(2, m) for m in range(2, 5)] + [(a, 9 - a) for a in range(5, 8)],
+GROUPS = {
+    "inner": [(INNER, [4, 5, 6, 7])],
+    NEAR: [([(3, m) for m in range(1, 5)] + [(a, 8 - a) for a in range(4, 8)], [3, 8])],
+    OTHER: [([(2, 4), (5, 4)], [2, 9]), ([(2, 2), (2, 3), (6, 3), (7, 2)], [])],
 }
-FAR = {NEAR: [3, 8], OTHER: [2, 9]}
+SHIPPED = {"next": [(4, 4), (5, 3), (5, 4)], "prev": [(3, 3), (3, 4), (2, 4)]}
+TAIL = {"next": (5, 4), "prev": (2, 4)}
+TAIL_BLOCKS = 2
 
 
 def slot(a, m):
@@ -41,29 +47,27 @@
 
 PLACE = {}
 POWER = {}
-SPAN = {}
-
-
-def give_places(name, edges, dates):
-    first = 2 * len(PLACE) + len(POWER)
-    for edge in edges:
-        PLACE[edge] = 2 * len(PLACE) + len(POWER)
-    for date in dates:
-        POWER[date] = 2 * len(PLACE) + len(POWER)
-    SPAN[name] = (first, 2 * len(PLACE) + len(POWER) - first)
-
-
-give_places("inner", INNER, [4, 5, 6, 7])
-give_places(NEAR, CROSS[NEAR], FAR[NEAR])
-give_places(OTHER, CROSS[OTHER], FAR[OTHER])
-N_ALL = SPAN[OTHER][0] + SPAN[OTHER][1]
-SHIPPED = {"next": [(4, 4), (5, 3), (5, 4)], "prev": [(3, 3), (3, 4), (2, 4)]}
+N_ALL = 0
+for _groups in GROUPS.values():
+    for _edges, _dates in _groups:
+        for _edge in _edges:
+            PLACE[_edge] = N_ALL
+            N_ALL += 2
+        for _date in _dates:
+            POWER[_date] = N_ALL
+            N_ALL += 1
+
+
+def edges_of(name):
+    return [edge for edges, _ in GROUPS[name] for edge in edges]
 
 
 def kernel(
     partner_offset, slc, interferogram, coherence,
-    offsets, own, far, own_wide, far_wide, sel, sums, edge_sums, halo, relayed, results,
+    offsets, own, far, own_wide, far_wide, sel, sums, edge_sums, halo, relayed, results, tail,
+    extra, extra_wide, lent, borrowed,
     offset_sem, own_sem, send_sem, recv_sem, halo_send, halo_recv, relay_send, relay_recv, ship_send, ship_recv,
+    tail_send, tail_recv, extra_sem, lend_sem,
 ):
     rows = own.shape[2]
     cells = own.shape[3]
@@ -97,6 +101,10 @@
     later = {"prev": false, "next": false, "low": false, "high": remote["high"]}
     former = {"prev": false, "next": false, "low": remote["low"], "high": false}
 
+    turn = lax.axis_size("date") // 4
+    early = (d % turn == 0) & (d > 0)
+    late = (d % turn == turn - 1) & has["next"]
+
     def own_copy(step):
         part = (slice(None), slice(None), pl.ds(step * INNER_ROWS, INNER_ROWS))
         return pltpu.make_async_copy(slc.at[part], own.at[part], own_sem.at[step])
@@ -126,6 +134,46 @@
             device_id_type=MESH,
         )
 
+    def extra_copy():
+        return pltpu.make_async_remote_copy(
+            src_ref=slc.at[:, pl.ds(1, 1), pl.ds(UNITS[SHIFT][0], UNITS[SHIFT][1])],
+            dst_ref=extra,
+            send_sem=extra_sem.at[0],
+            recv_sem=extra_sem.at[1],
+            device_id=where["next"],
+            device_id_type=MESH,
+        )
+
+    def lend_copy():
+        return pltpu.make_async_remote_copy(
+            src_ref=lent,
+            dst_ref=borrowed,
+            send_sem=lend_sem.at[0],
+            recv_sem=lend_sem.at[1],
+            device_id=where["prev"],
+            device_id_type=MESH,
+        )
+
+    def tail_copy(side):
+        n = 0 if side == "next" else 1
+        return pltpu.make_async_remote_copy(
+            src_ref=results.at[slot(*TAIL[side]), :, pl.ds(0, TAIL_BLOCKS * BLOCK)],
+            dst_ref=tail.at[n],
+            send_sem=tail_send.at[n],
+            recv_sem=tail_recv.at[n],
+            device_id=where[side],
+            device_id_type=MESH,
+        )
+
+    def goes(side, unit):
+        return has[side] & jnp.logical_not(early) if (side, unit) == ("prev", SHIFT) else has[side]
+
+    def comes(side, unit):
+        return has[side] & jnp.logical_not(late) if (side, unit) == ("next", SHIFT) else has[side]
+
+    def ships(side, edge, block):
+        return edge in SHIPPED[side] and not (edge == TAIL[side] and block < TAIL_BLOCKS)
+
     def ship_copy(side, edge, block):
         a, m = edge
         n, shift = (0, -16) if side == "next" else (1, 16)
@@ -140,20 +188,20 @@
             device_id_type=MESH,
         )
 
+    barrier = pltpu.get_barrier_semaphore()
+
+    def count(flags):
+        return sum(flag.astype(jnp.int32) for flag in flags)
+
+    for side in has:
+        @pl.when(greets[side] & jnp.logical_not(later[side] | former[side]))
+        def _(side=side):
+            pl.semaphore_signal(barrier, inc=1, device_id=where[side], device_id_type=MESH)
+
     offset_copy = pltpu.make_async_copy(partner_offset, offsets, offset_sem)
     for step in range(rows // INNER_ROWS):
         own_copy(step).start()
     offset_copy.start()
-
-    barrier = pltpu.get_barrier_semaphore()
-
-    def count(flags):
-        return sum(flag.astype(jnp.int32) for flag in flags)
-
-    for side in has:
-        @pl.when(greets[side] & jnp.logical_not(later[side] | former[side]))
-        def _(side=side):
-            pl.semaphore_signal(barrier, inc=1, device_id=where[side], device_id_type=MESH)
 
     look = lax.broadcasted_iota(jnp.int32, (128, columns), 1)
     cell = lax.broadcasted_iota(jnp.int32, (128, columns), 0)
@@ -170,9 +218,13 @@
 
     def send(unit):
         for side in ("next", "prev"):
-            @pl.when(has[side])
+            @pl.when(goes(side, unit))
             def _(side=side):
                 image_copy(side, unit).start()
+        if unit == SHIFT:
+            @pl.when(late)
+            def _():
+                extra_copy().start()
 
     for unit in range(IN_FLIGHT):
         send(unit)
@@ -184,6 +236,14 @@
             base = 3 if side == "prev" else 27
             results[base] = jnp.zeros(results.shape[1:], results.dtype)
             results[pl.ds(base + 3, 2)] = jnp.zeros((2,) + results.shape[1:], results.dtype)
+            tail[n] = jnp.zeros(tail.shape[1:], tail.dtype)
+    for side in range(2):
+        part = pl.ds(0, TAIL_BLOCKS * BLOCK)
+        results[(7, 27)[side], :, part] = jnp.zeros(tail.shape[1:], results.dtype)
+    @pl.when(late)
+    def _():
+        rows_of = pl.ds(UNITS[SHIFT][0], UNITS[SHIFT][1])
+        far[1, :, 1, rows_of] = jnp.zeros((2, UNITS[SHIFT][1], cells), far.dtype)
     for side, n in (("low", 0), ("high", 1)):
         @pl.when(jnp.logical_not(has[side]))
         def _(n=n):
@@ -197,11 +257,11 @@
 
         lax.fori_loop(0, cells // 128, body, 0, unroll=2)
 
-    def add_up(base, far_base, height, edges, dates, first, count):
+    def add_up(base, far_base, height, groups, output=None):
         pairs = height // 2
-        groups = edges if dates is None else [(edges, dates)]
-        every = [e for pairs_of, _ in groups for e in pairs_of]
-        needed = sorted({a for a, m in every} | {a + m for a, m in every})
+        first = PLACE.get(groups[0][0][0])
+        count = sum(2 * len(edges) + len(dates) for edges, dates in groups)
+        needed = sorted({b for edges, _ in groups for a, m in edges for b in (a, a + m)})
 
         def body(k, total):
             packed = []
@@ -216,6 +276,8 @@
                             row = pl.ds((base if 4 <= a < 8 else far_base) + odd, pairs, stride=2)
                             if 4 <= a < 8:
                                 value[a].append(own_wide[c, a - 4, tile, row])
+                            elif a == 1:
+                                value[a].append(extra_wide[c, 0, tile, row])
                             elif a < 4:
                                 value[a].append(far_wide[0, c, a - 2, tile, row])
                             else:
@@ -239,7 +301,11 @@
             return total + jnp.dot(left, right, preferred_element_type=jnp.float32)
 
         total = lax.fori_loop(0, cells // LANES, body, jnp.zeros((count * pairs, columns), jnp.float32))
-        sums[pl.ds(first, count), pl.ds(PAD + base // 2, pairs), :] = total.reshape(count, pairs, columns)
+        total = total.reshape(count, pairs, columns)
+        if output is None:
+            sums[pl.ds(first, count), pl.ds(PAD + base // 2, pairs), :] = total
+        else:
+            output[pl.ds(0, count)] = total
 
     def windows(q, block):
         base = PAD + block * BLOCK * 2
@@ -267,7 +333,7 @@
         own_copy(step).wait()
         row = pl.ds(step * INNER_ROWS, INNER_ROWS)
         widen(own, own_wide.at[:, :, :, row], row)
-        add_up(step * INNER_ROWS, 0, INNER_ROWS, INNER, [4, 5, 6, 7], *SPAN["inner"])
+        add_up(step * INNER_ROWS, 0, INNER_ROWS, GROUPS["inner"])
 
     @pl.when(greets["high"] & later["high"])
     def _():
@@ -321,40 +387,73 @@
             sums[q, pl.ds(PAD + rows // 2, 1)] = halo[1, pl.ds(q, 1)]
 
     def finish_block(name, block):
-        edges = INNER if name == "inner" else CROSS[name]
         power = {}
+        edges = edges_of(name)
         for side in ("next", "prev"):
-            owed = [e for e in edges if e in SHIPPED[side]]
+            owed = [edge for edge in edges if ships(side, edge, block)]
             finish(block, owed, power)
             if owed:
                 @pl.when(has[side])
                 def _(side=side, owed=owed):
                     for edge in owed:
                         ship_copy(side, edge, block).start()
-        finish(block, [e for e in edges if e not in SHIPPED["next"] + SHIPPED["prev"]], power)
+        done = SHIPPED["next"] + SHIPPED["prev"]
+        finish(block, [edge for edge in edges if edge not in done], power)
+
+    def lend():
+        first, height, _ = UNITS[SHIFT]
+        extra_copy().wait_recv()
+        widen(extra, extra_wide, pl.ds(0, height))
+        add_up(first, 0, height, [([(1, 4)], [])], lent)
+        row = pl.ds(PAD + first // 2, height // 2)
+        for i, edge in enumerate(((2, 3), (3, 2))):
+            lent[pl.ds(2 + 2 * i, 2)] = sums[pl.ds(PLACE[edge], 2), row]
+        lent[6] = sums[POWER[5], row]
+        lend_copy().start()
+
+    def borrow():
+        first, height, _ = UNITS[SHIFT]
+        lend_copy().wait_recv()
+        row = pl.ds(PAD + first // 2, height // 2)
+        for i, edge in enumerate(((5, 4), (6, 3), (7, 2))):
+            sums[pl.ds(PLACE[edge], 2), row] = borrowed[pl.ds(2 * i, 2)]
+        sums[POWER[9], row] = borrowed[6]
 
     ready = {"inner": set(range(rows)), NEAR: set(), OTHER: set()}
     finished = set()
     for unit, (first, height, dates) in enumerate(UNITS):
         for side in ("prev", "next"):
-            @pl.when(has[side])
+            @pl.when(comes(side, unit))
             def _(side=side):
                 image_copy("next" if side == "prev" else "prev", unit).wait_recv()
         if unit + IN_FLIGHT < len(UNITS):
             send(unit + IN_FLIGHT)
         if unit == HALO_AT:
             take_halo()
-        row = pl.ds(first, height)
+        if unit == BORROW_AT:
+            pl.when(late)(borrow)
+            ready[OTHER] |= set(range(UNITS[SHIFT][0], UNITS[SHIFT][0] + UNITS[SHIFT][1]))
         for side, (low, high) in ((0, (2 - dates[1], 2 - dates[0])), (1, dates)):
             date = pl.ds(low, high - low)
-            widen(far.at[side, :, date], far_wide.at[side, :, date, :, pl.ds(0, height)], row)
+            widen(far.at[side, :, date], far_wide.at[side, :, date, :, pl.ds(0, height)], pl.ds(first, height))
         names = [name for name in (NEAR, OTHER) if dates[0] <= name[0] and name[1] <= dates[1]]
-        begin = SPAN[names[0]][0]
-        number = sum(SPAN[name][1] for name in names)
-        edges = [(CROSS[name], FAR[name]) for name in names]
-        add_up(first, 0, height, edges, None, begin, number)
+        if unit == LAST:
+            add_up(first, 0, height, GROUPS[OTHER][:1])
+            power = {}
+            for side in ("next", "prev"):
+                for block in range(TAIL_BLOCKS):
+                    finish(block, [TAIL[side]], power.setdefault(block, {}))
+                @pl.when(has[side])
+                def _(side=side):
+                    tail_copy(side).start()
+            add_up(first, 0, height, GROUPS[OTHER][1:])
+        else:
+            add_up(first, 0, height, [group for name in names for group in GROUPS[name]])
         for name in names:
-            ready[name] |= set(range(first, first + height))
+            if unit != SHIFT:
+                ready[name] |= set(range(first, first + height))
+        if unit == SHIFT:
+            pl.when(early)(lend)
         if unit == EDGES_AT:
             send_edges()
         if unit == RELAY_AT[0]:
@@ -367,8 +466,8 @@
                     height_of = BLOCK * LOOK_AZ
                     reach = set(range(max(block * height_of - 2, 0), min((block + 1) * height_of + 2, rows)))
                     inside = 0 < block < blocks - 1
-                    late = (0 if name == "inner" else SHIP_AT) if inside else HALO_AT
-                    if (name, block) not in finished and reach <= ready[name] and unit >= late:
+                    least = (0 if name == "inner" else SHIP_AT) if inside else HALO_AT
+                    if (name, block) not in finished and reach <= ready[name] and unit >= least:
                         finish_block(name, block)
                         finished.add((name, block))
 
@@ -377,27 +476,53 @@
         def _(side=side, opposite=opposite):
             for block in range(blocks):
                 for edge in SHIPPED[opposite]:
-                    ship_copy(opposite, edge, block).wait_recv()
+                    if ships(opposite, edge, block):
+                        ship_copy(opposite, edge, block).wait_recv()
 
     offset_copy.wait()
+    places = {}
     for i in range(OWN):
         for k in range(4):
             offset = offsets[i, k]
             place = 4 * (OWN + i + jnp.minimum(offset, 0)) + jnp.abs(offset) - 1
             sign = jnp.where(offset > 0, 1.0, -1.0)
+            places[i, k] = place
             chosen = results[place]
             interferogram[i, k, 0] = chosen[0]
             interferogram[i, k, 1] = chosen[1] * sign
             coherence[i, k] = chosen[2]
 
+    for n, side, i, sign in ((0, "prev", 1, -1.0), (1, "next", 2, 1.0)):
+        @pl.when(has[side])
+        def _(side=side):
+            tail_copy("next" if side == "prev" else "prev").wait_recv()
+        part = pl.ds(0, TAIL_BLOCKS * BLOCK)
+        for k in range(4):
+            here = places[i, k] == (7, 27)[n]
+            interferogram[i, k, 0, part] = jnp.where(here, tail[n, 0], interferogram[i, k, 0, part])
+            interferogram[i, k, 1, part] = jnp.where(here, tail[n, 1] * sign, interferogram[i, k, 1, part])
+            coherence[i, k, part] = jnp.where(here, tail[n, 2], coherence[i, k, part])
+
     for side in ("next", "prev"):
         @pl.when(has[side])
         def _(side=side):
             for unit in range(len(UNITS)):
-                image_copy(side, unit).wait_send()
+                if (side, unit) != ("prev", SHIFT):
+                    image_copy(side, unit).wait_send()
+            tail_copy(side).wait_send()
             for block in range(blocks):
                 for edge in SHIPPED[side]:
-                    ship_copy(side, edge, block).wait_send()
+                    if ships(side, edge, block):
+                        ship_copy(side, edge, block).wait_send()
+    @pl.when(goes("prev", SHIFT))
+    def _():
+        image_copy("prev", SHIFT).wait_send()
+    @pl.when(late)
+    def _():
+        extra_copy().wait_send()
+    @pl.when(early)
+    def _():
+        lend_copy().wait_send()
     for side, n in (("high", 0), ("low", 1)):
         @pl.when(has[side] & (inner | jnp.logical_not(remote[side])))
         def _(side=side, n=n):
@@ -437,6 +562,11 @@
             pltpu.VMEM((2, N_ALL, columns), f32),
             pltpu.VMEM((2, N_ALL, columns), f32),
             pltpu.VMEM((32, 3, looks, columns), f32),
+            pltpu.VMEM((2, 3, TAIL_BLOCKS * BLOCK, columns), f32),
+            pltpu.VMEM((2, 1, UNITS[SHIFT][1], cells), slc.dtype),
+            pltpu.VMEM((2, 1, cells // 128, UNITS[SHIFT][1], 128), f32),
+            pltpu.VMEM((7, UNITS[SHIFT][1] // 2, columns), f32),
+            pltpu.VMEM((7, UNITS[SHIFT][1] // 2, columns), f32),
             pltpu.SemaphoreType.DMA,
             pltpu.SemaphoreType.DMA((steps,)),
             pltpu.SemaphoreType.DMA((2, len(UNITS))),
@@ -447,6 +577,10 @@
             pltpu.SemaphoreType.DMA((2,)),
             pltpu.SemaphoreType.DMA((2, 3, blocks)),
             pltpu.SemaphoreType.DMA((2, 3, blocks)),
+            pltpu.SemaphoreType.DMA((2,)),
+            pltpu.SemaphoreType.DMA((2,)),
+            pltpu.SemaphoreType.DMA((2,)),
+            pltpu.SemaphoreType.DMA((2,)),
         ],
         compiler_params=pltpu.CompilerParams(
             collective_id=0, has_side_effects=True, vmem_limit_bytes=211 * 1024 * 256

time: 67.4 us -> 65.2 us (0.967)
  Pallas kernels: 64.5 us -> 61.8 us
    pallas_call x1, Pallas kernels: 64.5 us -> 61.8 us  [per_device(): pl.pallas_call(kernel, out_shape=(jax.ShapeDtypeStruct((dates, 4, 2, look...]
where the time goes in v4:
time: 65.2 us; the launch traced here: 64.6 us
  Pallas kernels  61.8 us (95%)
  local copies, waits for them, and re-layouts  2.17 us (3%)
    pallas_call x1, Pallas kernels, per_device(): pl.pallas_call(kernel, out_shape=(jax.ShapeDtypeStruct((dates, 4, 2, look...  61.8 us
    unnamed x4, local copies, waits for them, and re-layouts  2.17 us

profile of v4, /device:TPU:6, one launch (start us, length us, event | category | flops | bytes accessed | tf_op | source)
XLA Modules:
  0.0 64.6 jit_solution(14941552799248774176)
XLA Ops:
  0.6 0.0 copy-start
  0.6 0.7 %copy-done = s32[4,4]{1,0:T(4,128)S(1)} copy-done((s32[4,4]{1,0:T(4,128)S(1)}, s32[4,4]{1,0:T(4,128)}, u32[]{:S(2)}) %copy-start) | copy-done | bytes 88
  1.3 61.8 %shard_map.41 = (f32[4,4,2,32,128]{4,3,2,1,0:T(8,128)S(1)}, f32[4,4,32,128]{3,2,1,0:T(8,128)S(1)}) custom-call(s32[4,4]{1,0:T(4,128)S(1)} %copy-done, bf16[2,4,128,2048]{3,2,1,0:T(8,128)(2,1)} %slc.1), custom_call_target="tpu_custom_call" | custom-call | tf_op jit(solution)/shard_map/pallas_call | solution.py:542
  63.1 0.8 %copy.6 = f32[4,4,2,32,128]{4,3,2,1,0:T(8,128)} copy(f32[4,4,2,32,128]{4,3,2,1,0:T(8,128)S(1)} %get-tuple-element.4) | data formatting | bytes 1048576
  63.9 0.7 %copy.7 = f32[4,4,32,128]{3,2,1,0:T(8,128)} copy(f32[4,4,32,128]{3,2,1,0:T(8,128)S(1)} %get-tuple-element.5) | data formatting | bytes 524288
Async XLA Ops:
  0.6 0.7 %copy-start = (s32[4,4]{1,0:T(4,128)S(1)}, s32[4,4]{1,0:T(4,128)}, u32[]{:S(2)}) copy-start(s32[4,4]{1,0:T(4,128)} %partner_offset.1) | copy-start | bytes 196

commit v5 on v4

--- a/solution.py
+++ b/solution.py
@@ -17,7 +17,8 @@
 INNER_ROWS = 32
 PAD = 8
 BLOCK = 8
-IN_FLIGHT = 3
+IN_FLIGHT = (3, 2)
+CATCH_UP = 3
 BOTH, NEAR, OTHER = (0, 2), (0, 1), (1, 2)
 UNITS = [(0, 16, BOTH), (112, 16, BOTH)]
 UNITS += [(16, 32, NEAR), (48, 32, NEAR), (80, 32, NEAR)]
@@ -28,7 +29,7 @@
 SHIFT = 5
 BORROW_AT = 7
 SHIP_AT = 7
-HALO_AT = 8
+HALO_AT = 7
 
 INNER = [(a, m) for a in range(4, 8) for m in range(1, 5) if a + m < 8]
 GROUPS = {
@@ -102,8 +103,9 @@
     former = {"prev": false, "next": false, "low": remote["low"], "high": false}
 
     turn = lax.axis_size("date") // 4
-    early = (d % turn == 0) & (d > 0)
-    late = (d % turn == turn - 1) & has["next"]
+    shifts = s < lax.axis_size("strip") // 2
+    early = (d % turn == 0) & (d > 0) & shifts
+    late = (d % turn == turn - 1) & has["next"] & shifts
 
     def own_copy(step):
         part = (slice(None), slice(None), pl.ds(step * INNER_ROWS, INNER_ROWS))
@@ -216,18 +218,20 @@
         def _(side=side):
             pl.semaphore_signal(barrier, inc=1, device_id=where[side], device_id_type=MESH)
 
-    def send(unit):
+    def send(unit, device):
         for side in ("next", "prev"):
-            @pl.when(goes(side, unit))
+            @pl.when(goes(side, unit) & (s % 2 == device))
             def _(side=side):
                 image_copy(side, unit).start()
         if unit == SHIFT:
-            @pl.when(late)
+            @pl.when(late & (s % 2 == device))
             def _():
                 extra_copy().start()
 
-    for unit in range(IN_FLIGHT):
-        send(unit)
+    for device in range(2):
+        for unit in range(IN_FLIGHT[device]):
+            send(unit, device)
+    started = list(IN_FLIGHT)
 
     for side, n in (("prev", 0), ("next", 1)):
         @pl.when(jnp.logical_not(has[side]))
@@ -426,8 +430,11 @@
             @pl.when(comes(side, unit))
             def _(side=side):
                 image_copy("next" if side == "prev" else "prev", unit).wait_recv()
-        if unit + IN_FLIGHT < len(UNITS):
-            send(unit + IN_FLIGHT)
+        for device in range(2):
+            ahead = IN_FLIGHT[0 if unit >= CATCH_UP else device]
+            while started[device] < min(unit + 1 + ahead, len(UNITS)):
+                send(started[device], device)
+                started[device] += 1
         if unit == HALO_AT:
             take_halo()
         if unit == BORROW_AT:
@@ -466,7 +473,7 @@
                     height_of = BLOCK * LOOK_AZ
                     reach = set(range(max(block * height_of - 2, 0), min((block + 1) * height_of + 2, rows)))
                     inside = 0 < block < blocks - 1
-                    least = (0 if name == "inner" else SHIP_AT) if inside else HALO_AT
+                    least = (0 if inside else LAST) if name == "inner" else (SHIP_AT if inside else HALO_AT)
                     if (name, block) not in finished and reach <= ready[name] and unit >= least:
                         finish_block(name, block)
                         finished.add((name, block))

time: 65.2 us -> 64.6 us (level)
  Pallas kernels: 61.8 us -> 61 us
    pallas_call x1, Pallas kernels: 61.8 us -> 61 us  [per_device(): pl.pallas_call(kernel, out_shape=(jax.ShapeDtypeStruct((dates, 4, 2, look...]
where the time goes in v5:
time: 64.6 us; the launch traced here: 63.8 us
  Pallas kernels  61 us (94%)
  local copies, waits for them, and re-layouts  2.17 us (3%)
  between operations  0.65 us (1%)
    pallas_call x1, Pallas kernels, per_device(): pl.pallas_call(kernel, out_shape=(jax.ShapeDtypeStruct((dates, 4, 2, look...  61 us
    unnamed x4, local copies, waits for them, and re-layouts  2.17 us

profile of v5, /device:TPU:6, one launch (start us, length us, event | category | flops | bytes accessed | tf_op | source)
XLA Modules:
  0.0 63.8 jit_solution(8357715668512803582)
XLA Ops:
  0.6 0.0 copy-start
  0.6 0.7 %copy-done = s32[4,4]{1,0:T(4,128)S(1)} copy-done((s32[4,4]{1,0:T(4,128)S(1)}, s32[4,4]{1,0:T(4,128)}, u32[]{:S(2)}) %copy-start) | copy-done | bytes 88
  1.3 61.0 %shard_map.41 = (f32[4,4,2,32,128]{4,3,2,1,0:T(8,128)S(1)}, f32[4,4,32,128]{3,2,1,0:T(8,128)S(1)}) custom-call(s32[4,4]{1,0:T(4,128)S(1)} %copy-done, bf16[2,4,128,2048]{3,2,1,0:T(8,128)(2,1)} %slc.1), custom_call_target="tpu_custom_call" | custom-call | tf_op jit(solution)/shard_map/pallas_call | solution.py:549
  62.3 0.8 %copy.6 = f32[4,4,2,32,128]{4,3,2,1,0:T(8,128)} copy(f32[4,4,2,32,128]{4,3,2,1,0:T(8,128)S(1)} %get-tuple-element.4) | data formatting | bytes 1048576
  63.1 0.7 %copy.7 = f32[4,4,32,128]{3,2,1,0:T(8,128)} copy(f32[4,4,32,128]{3,2,1,0:T(8,128)S(1)} %get-tuple-element.5) | data formatting | bytes 524288
Async XLA Ops:
  0.6 0.7 %copy-start = (s32[4,4]{1,0:T(4,128)S(1)}, s32[4,4]{1,0:T(4,128)}, u32[]{:S(2)}) copy-start(s32[4,4]{1,0:T(4,128)} %partner_offset.1) | copy-start | bytes 196

commit v6 on v5

--- a/solution.py
+++ b/solution.py
@@ -35,7 +35,7 @@
 GROUPS = {
     "inner": [(INNER, [4, 5, 6, 7])],
     NEAR: [([(3, m) for m in range(1, 5)] + [(a, 8 - a) for a in range(4, 8)], [3, 8])],
-    OTHER: [([(2, 4), (5, 4)], [2, 9]), ([(2, 2), (2, 3), (6, 3), (7, 2)], [])],
+    OTHER: [([(5, 4)], [9]), ([(2, 4)], [2]), ([(2, 2), (2, 3), (6, 3), (7, 2)], [])],
 }
 SHIPPED = {"next": [(4, 4), (5, 3), (5, 4)], "prev": [(3, 3), (3, 4), (2, 4)]}
 TAIL = {"next": (5, 4), "prev": (2, 4)}
@@ -426,7 +426,7 @@
     ready = {"inner": set(range(rows)), NEAR: set(), OTHER: set()}
     finished = set()
     for unit, (first, height, dates) in enumerate(UNITS):
-        for side in ("prev", "next"):
+        for side in ("prev", "next") if unit < LAST else ():
             @pl.when(comes(side, unit))
             def _(side=side):
                 image_copy("next" if side == "prev" else "prev", unit).wait_recv()
@@ -440,20 +440,27 @@
         if unit == BORROW_AT:
             pl.when(late)(borrow)
             ready[OTHER] |= set(range(UNITS[SHIFT][0], UNITS[SHIFT][0] + UNITS[SHIFT][1]))
-        for side, (low, high) in ((0, (2 - dates[1], 2 - dates[0])), (1, dates)):
+        def widen_side(side):
+            low, high = dates if side else (2 - dates[1], 2 - dates[0])
             date = pl.ds(low, high - low)
             widen(far.at[side, :, date], far_wide.at[side, :, date, :, pl.ds(0, height)], pl.ds(first, height))
+
+        for side in range(2) if unit < LAST else ():
+            widen_side(side)
         names = [name for name in (NEAR, OTHER) if dates[0] <= name[0] and name[1] <= dates[1]]
         if unit == LAST:
-            add_up(first, 0, height, GROUPS[OTHER][:1])
-            power = {}
-            for side in ("next", "prev"):
+            for n, (side, source) in enumerate((("next", "prev"), ("prev", "next"))):
+                @pl.when(has[side])
+                def _(source=source):
+                    image_copy(source, unit).wait_recv()
+                widen_side(1 - n)
+                add_up(first, 0, height, GROUPS[OTHER][n : n + 1])
                 for block in range(TAIL_BLOCKS):
-                    finish(block, [TAIL[side]], power.setdefault(block, {}))
+                    finish(block, [TAIL[side]], {})
                 @pl.when(has[side])
                 def _(side=side):
                     tail_copy(side).start()
-            add_up(first, 0, height, GROUPS[OTHER][1:])
+            add_up(first, 0, height, GROUPS[OTHER][2:])
         else:
             add_up(first, 0, height, [group for name in names for group in GROUPS[name]])
         for name in names:

time: 64.6 us -> 64.5 us (level)
  no operation moved by 1% of the time
where the time goes in v6:
time: 64.5 us; the launch traced here: 63.7 us
  Pallas kernels  60.9 us (94%)
  local copies, waits for them, and re-layouts  2.17 us (3%)
  between operations  0.65 us (1%)
    pallas_call x1, Pallas kernels, per_device(): pl.pallas_call(kernel, out_shape=(jax.ShapeDtypeStruct((dates, 4, 2, look...  60.9 us
    unnamed x4, local copies, waits for them, and re-layouts  2.17 us

profile of v6, /device:TPU:6, one launch (start us, length us, event | category | flops | bytes accessed | tf_op | source)
XLA Modules:
  0.0 63.7 jit_solution(1014113144103130590)
XLA Ops:
  0.6 0.0 copy-start
  0.6 0.7 %copy-done = s32[4,4]{1,0:T(4,128)S(1)} copy-done((s32[4,4]{1,0:T(4,128)S(1)}, s32[4,4]{1,0:T(4,128)}, u32[]{:S(2)}) %copy-start) | copy-done | bytes 88
  1.3 60.9 %shard_map.41 = (f32[4,4,2,32,128]{4,3,2,1,0:T(8,128)S(1)}, f32[4,4,32,128]{3,2,1,0:T(8,128)S(1)}) custom-call(s32[4,4]{1,0:T(4,128)S(1)} %copy-done, bf16[2,4,128,2048]{3,2,1,0:T(8,128)(2,1)} %slc.1), custom_call_target="tpu_custom_call" | custom-call | tf_op jit(solution)/shard_map/pallas_call | solution.py:556
  62.2 0.8 %copy.6 = f32[4,4,2,32,128]{4,3,2,1,0:T(8,128)} copy(f32[4,4,2,32,128]{4,3,2,1,0:T(8,128)S(1)} %get-tuple-element.4) | data formatting | bytes 1048576
  63.0 0.7 %copy.7 = f32[4,4,32,128]{3,2,1,0:T(8,128)} copy(f32[4,4,32,128]{3,2,1,0:T(8,128)S(1)} %get-tuple-element.5) | data formatting | bytes 524288
Async XLA Ops:
  0.6 0.7 %copy-start = (s32[4,4]{1,0:T(4,128)S(1)}, s32[4,4]{1,0:T(4,128)}, u32[]{:S(2)}) copy-start(s32[4,4]{1,0:T(4,128)} %partner_offset.1) | copy-start | bytes 196
